TPU v7x, 32 devices: a whole 2x2x4 slice. The times are simulated.
32 devices in a mesh: blk: 8 (over z, y), lblk: 4 (over x, core).
Axes of the slice: x: 2, y: 2, z: 4, core: 2. Of those that a mesh axis runs over, the one named last changes fastest.
Arguments:
- partial_rows: bfloat16 [4, 8192, 1024], P('lblk', 'blk'), may hold values from -5 to 5
- row_owner: int32 [4, 8192, 1], P('lblk', 'blk'), may hold values from 0 to 7; in each aligned block of 1024 rows (0 to 1023, 1024 to 2047, ..., all dimensions but the last counted through in order) at most 128 rows name the same one
- row_key: int32 [4, 8192], P('lblk', 'blk'), may hold values from 0 to 127
- azimuth_orders: int32 [8], replicated, may hold values from 1 to 4095, as said below
- legendre_table: bfloat16 [8, 4096, 256], P('blk', 'lblk'), may hold values from -0.375 to 0.375
- spin_even: bfloat16 [8, 4096, 256], P('blk', 'lblk'), may hold values from -0.375 to 0.375
- spin_odd: bfloat16 [8, 4096, 256], P('blk', 'lblk'), may hold values from -0.375 to 0.375
Outputs:
- eigenvalues: float32 [2, 2, 4, 64, 8192], P(None, None, 'lblk', 'blk')
- cycle_maps: float32 [2, 4, 64, 8192], P(None, 'lblk', 'blk')
Inputs may be any that keep to these rules, and one draw needn't show every extreme that they name: `row_owner`: no more than 128 rows of one device name the same owner; some device sends exactly 128 rows to some owner in every draw. `azimuth_orders`: all distinct; 1 and 4095 are always among them.
All inputs are finite; a program needn't handle non-finite values.
Results may differ from a plain program's by a relative error of at most 0.0041.
Values may be sent and summed in bfloat16 or wider, within the bound.
A program may use at most 128 MiB of HBM per device.

v0:
```python
import math

import jax
import jax.numpy as jnp
from jax import lax
from jax.sharding import PartitionSpec as P

NPHI = 8192
L = 4096
SEG = 1024
R_DEV = 8
PR = 1024
KEYS = 128
CAP = 128


def wave_table(azimuth_orders, length):
    orders = azimuth_orders.shape[0]
    phase_index = (
        lax.broadcasted_iota(jnp.int32, (orders, length), 1) * azimuth_orders[:, None] % length
    )
    angles = phase_index.astype(jnp.float32) * (2.0 * math.pi / length)
    return jnp.concatenate([jnp.cos(angles), jnp.sin(angles)], axis=0)


def degree_factors(degree):
    smoothing = jnp.exp(-2.0 * degree * (degree + 1.0) / (L * L))
    factor = jnp.sqrt(
        jnp.maximum((degree - 1.0) * (degree + 2.0), 0.0)
        / jnp.maximum(degree * (degree + 1.0), 1.0)
    )
    return (smoothing, factor)


def eigen_pair(coefficients, waves):
    orders = coefficients.shape[1]
    real_part = coefficients[..., 0]
    imag_part = coefficients[..., 1]
    real_all = jnp.concatenate([real_part[:, :, :2], -imag_part[:, :, 2:]], axis=2)
    imag_all = jnp.concatenate([imag_part[:, :, :2], real_part[:, :, 2:]], axis=2)
    stacked = jnp.concatenate([real_all, -imag_all], axis=1)
    fields = lax.dot_general(
        stacked, waves, (((1,), (0,)), ((), ())), precision=lax.Precision.HIGHEST
    ) * (2.0 / math.sqrt(orders))
    half_trace = 0.5 * fields[:, 0]
    shear_size = jnp.sqrt(fields[:, 1] * fields[:, 1] + fields[:, 2] * fields[:, 2])
    return jnp.stack([half_trace + shear_size, half_trace - shear_size], axis=0)


def body(partial_rows, row_owner, row_key, azimuth_orders, legendre_table, spin_even, spin_odd):
    groups = lax.axis_size("blk")
    row_values = partial_rows[0]
    owners = row_owner[0, :, 0]
    pixel_keys = row_key[0]
    target = lax.broadcasted_iota(jnp.int32, (groups, PR), 0) == owners[None, :]
    ranking = jnp.cumsum(target.astype(jnp.int32), axis=1) - 1
    slot_index = owners * CAP + jnp.sum(jnp.where(target, ranking, 0), axis=0)
    picked = lax.broadcasted_iota(jnp.int32, (groups * CAP, PR), 0) == slot_index[None, :]
    send_rows = jnp.dot(
        picked.astype(jnp.bfloat16), row_values, preferred_element_type=jnp.float32
    ).astype(jnp.bfloat16)
    send_keys = jnp.sum(jnp.where(picked, pixel_keys[None, :] + 1, 0), axis=1) - 1
    received_rows, received_keys = (
        lax.all_to_all(
            send_rows.reshape(groups, CAP, SEG), "blk", split_axis=0, concat_axis=0, tiled=True
        ),
        lax.all_to_all(
            send_keys.reshape(groups, CAP), "blk", split_axis=0, concat_axis=0, tiled=True
        ),
    )
    selector = lax.broadcasted_iota(jnp.int32, (KEYS, groups * CAP), 0) == received_keys.reshape(
        1, groups * CAP
    )
    cycle_blocks = jnp.dot(
        selector.astype(jnp.bfloat16),
        received_rows.reshape(groups * CAP, SEG),
        preferred_element_type=jnp.float32,
    )
    cycle_maps = cycle_blocks.reshape(2 * R_DEV, NPHI)
    cycle_out = cycle_blocks.reshape(2, R_DEV, NPHI)[:, None]
    waves = wave_table(azimuth_orders, NPHI)
    orders = azimuth_orders.shape[0]
    spectra = lax.dot_general(
        cycle_maps, waves, (((1,), (1,)), ((), ())), precision=lax.Precision.HIGHEST
    ) / math.sqrt(NPHI)
    sign_flip = jnp.array([1.0, -1.0], jnp.float32).reshape(1, 1, 2, 1)
    spectra = spectra.reshape(2, R_DEV, 2, orders) * sign_flip
    harmonics = spectra.transpose(3, 0, 2, 1).reshape(orders, 4, R_DEV).astype(jnp.bfloat16)
    harmonics = lax.all_to_all(harmonics, "blk", split_axis=0, concat_axis=2, tiled=True)
    mode_rows = legendre_table.shape[0]
    block_width = legendre_table.shape[1]
    coefficients = jnp.einsum(
        "mlr,mcr->mlc",
        legendre_table,
        lax.all_gather(harmonics, "lblk", axis=2, tiled=True),
        preferred_element_type=jnp.float32,
    )
    degree = (
        lax.axis_index("lblk") * block_width + lax.broadcasted_iota(jnp.int32, (block_width,), 0)
    ).astype(jnp.float32)
    smoothing, factor = degree_factors(degree)
    trace_terms = (smoothing[None, :, None] * coefficients).astype(jnp.bfloat16)
    shear_terms = ((-0.5 * smoothing * factor)[None, :, None] * coefficients).astype(jnp.bfloat16)
    total_cycles = legendre_table.shape[2]
    own_cycles = total_cycles // lax.axis_size("lblk")
    pieces = [
        jnp.einsum("mlr,mlc->rmc", legendre_table, trace_terms, preferred_element_type=jnp.float32),
        jnp.einsum("mlr,mlc->rmc", spin_even, shear_terms, preferred_element_type=jnp.float32),
        jnp.einsum("mlr,mlc->rmc", spin_odd, shear_terms, preferred_element_type=jnp.float32),
    ]
    all_cycles_sum = lax.psum(
        jnp.stack(pieces, axis=2).reshape(total_cycles, mode_rows * 12), "lblk"
    )
    summed = lax.dynamic_slice_in_dim(
        all_cycles_sum, lax.axis_index("lblk") * own_cycles, own_cycles, 0
    )
    returned = lax.all_to_all(
        summed.astype(jnp.bfloat16).reshape(own_cycles, mode_rows, 12),
        "blk",
        split_axis=0,
        concat_axis=1,
        tiled=True,
    )
    eigen = eigen_pair(returned.astype(jnp.float32).reshape(R_DEV, orders, 3, 2, 2), waves)
    return (eigen.transpose(0, 2, 1, 3)[:, :, None], cycle_out)


def solution(mesh):
    return jax.shard_map(
        body,
        mesh=mesh,
        in_specs=(
            P("lblk", "blk", None),
            P("lblk", "blk", None),
            P("lblk", "blk"),
            P(),
            P("blk", "lblk", None),
            P("blk", "lblk", None),
            P("blk", "lblk", None),
        ),
        out_specs=(P(None, None, "lblk", "blk", None), P(None, "lblk", "blk", None)),
        check_vma=False,
    )
```

profile of v0, /device:TPU:0, one launch (start us, length us, event | category | flops | bytes accessed | tf_op | source)
XLA Modules:
  0.0 124.5 jit_solution(3006084223195587247)
XLA Ops:
  0.6 0.8 broadcast_multiply_fusion
  2.2 2.3 %reduce-window.6 = s32[8,8,128]{2,1,0:T(8,128)S(1)} reduce-window(s32[8,8,128]{2,1,0:T(8,128)S(1)} %fusion.24, s32[]{:T(128)} %constant.19.clone.1), window={size=1x1x128 pad=0_0x0_0x127_0}, to_apply=%region_0.0 | reduce-window | flops 1040384 | bytes 65540 | tf_op jit(solution)/shard_map/reduce-window
  7.4 7.3 %all-to-all-start = ((s32[8,1,128]{2,1,0:T(1,128)}), s32[8,1,128]{2,1,0:T(1,128)S(1)}, u32[]{:S(2)}, u32[]{:S(2)}) async-start(s32[8,1,128]{2,1,0:T(1,128)} %bitcast.4), calls=%async_computation | async-start | bytes 8192 | tf_op jit(solution)/shard_map/all_to_all | solution.py:67
  14.7 3.6 %fusion.3 = bf16[1024,1024]{1,0:T(8,128)(2,1)} fusion(bf16[1,1024,1024]{2,1,0:T(8,128)(2,1)S(1)} %copy-done, s32[1024]{0:T(1024)S(1)} %bitcast_add_fusion), kind=kOutput, calls=%fused_computation.6 | convolution fusion | flops 2149580800 | bytes 4198400 | tf_op jit(solution)/shard_map/dot_general | solution.py:59
  18.4 2.8 %all-to-all-done = s32[8,1,128]{2,1,0:T(1,128)S(1)} async-done(((s32[8,1,128]{2,1,0:T(1,128)}), s32[8,1,128]{2,1,0:T(1,128)S(1)}, u32[]{:S(2)}, u32[]{:S(2)}) %all-to-all-start) | async-done | bytes 4128 | tf_op jit(solution)/shard_map/all_to_all | solution.py:67
  21.1 4.5 %all-to-all-start.1 = ((bf16[8,128,1024]{2,1,0:T(8,128)(2,1)}), bf16[8,128,1024]{2,1,0:T(8,128)(2,1)}, u32[]{:S(2)}, u32[]{:S(2)}) async-start(bf16[8,128,1024]{2,1,0:T(8,128)(2,1)} %bitcast.86), calls=%async_computation.1 | async-start | bytes 4194304 | tf_op jit(solution)/shard_map/all_to_all | solution.py:64
  25.6 1.1 fusion.23
  26.7 46.0 %all-to-all-done.1 = bf16[8,128,1024]{2,1,0:T(8,128)(2,1)} async-done(((bf16[8,128,1024]{2,1,0:T(8,128)(2,1)}), bf16[8,128,1024]{2,1,0:T(8,128)(2,1)}, u32[]{:S(2)}, u32[]{:S(2)}) %all-to-all-start.1) | async-done | bytes 2097184 | tf_op jit(solution)/shard_map/all_to_all | solution.py:64
  72.7 2.1 %fusion.14 = f32[128,1024]{1,0:T(8,128)S(1)} fusion(bf16[1024,1024]{1,0:T(8,128)(2,1)} %bitcast.8, s32[1024]{0:T(1024)S(1)} %bitcast.97), kind=kOutput, calls=%fused_computation.27 | convolution fusion | flops 268566528 | bytes 2625536 | tf_op jit(solution)/shard_map/dot_general | solution.py:74
  74.7 0.9 reshape.206
  75.6 1.8 %convolution_multiply_fusion.1 = f32[16,16]{1,0:T(8,128)S(1)} fusion(f32[16,8192]{1,0:T(8,128)} %reshape.206, f32[8,8192]{1,0:T(8,128)S(1)} %get-tuple-element.21, f32[8,8192]{1,0:T(8,128)S(1)} %get-tuple-element.20), kind=kOutput, calls=%fused_computation.7 | convolution fusion | flops 25297152 | bytes 1049600 | tf_op jit(solution)/shard_map/dot_general | solution.py:83
  78.3 3.6 %all-to-all-start.2 = ((bf16[8,4,8]{2,1,0:T(4,128)(2,1)}), bf16[8,4,8]{2,1,0:T(4,128)(2,1)S(1)}, u32[]{:S(2)}, u32[]{:S(2)}) async-start(bf16[8,4,8]{2,1,0:T(4,128)(2,1)} %copy.60), calls=%async_computation.2 | async-start | bytes 16384 | tf_op jit(solution)/shard_map/all_to_all | solution.py:89
  81.9 6.5 %all-to-all-done.2 = bf16[8,4,8]{2,1,0:T(4,128)(2,1)S(1)} async-done(((bf16[8,4,8]{2,1,0:T(4,128)(2,1)}), bf16[8,4,8]{2,1,0:T(4,128)(2,1)S(1)}, u32[]{:S(2)}, u32[]{:S(2)}) %all-to-all-start.2) | async-done | bytes 544 | tf_op jit(solution)/shard_map/all_to_all | solution.py:89
  88.7 5.4 %all_gather.3 = bf16[1,4,256]{1,0,2:T(2,128)(2,1)S(1)} all-gather(bf16[1,4,64]{1,0,2:T(2,128)(2,1)S(1)} %copy.62), channel_id=1, replica_groups=mesh['blk'=8,'lblk'=4] {'lblk'}, dimensions={2}, use_global_device_ids=true | all-gather | bytes 2560 | tf_op jit(solution)/shard_map/all_gather | solution.py:95
  94.2 1.3 %fusion.12 = f32[4,1024]{1,0:T(4,128)S(1)} fusion(bf16[1,1024,256]{2,1,0:T(8,128)(2,1)} %param.12, bf16[1,4,256]{2,1,0:T(4,128)(2,1)S(1)} %copy.63), kind=kOutput, calls=%fused_computation.22 | convolution fusion | flops 2097152 | bytes 542720 | tf_op jit(solution)/shard_map/mlr,mcr->mlc/dot_general | solution.py:92
  95.5 1.2 convolution_bitcast_fusion
  96.7 1.2 convolution_bitcast_fusion.1
  97.9 1.2 convolution_bitcast_fusion.2
  99.2 11.5 %psum.7 = bf16[256,12]{0,1:T(8,128)(2,1)S(1)} all-reduce(f32[256,12]{0,1:T(8,128)S(1)} %reshape.212), channel_id=1, replica_groups=mesh['blk'=8,'lblk'=4] {'lblk'}, use_global_device_ids=true, to_apply=%region_4.5 | all-reduce | flops 3072 | bytes 18432 | tf_op jit(solution)/shard_map/psum | solution.py:111
  111.4 3.3 %all-to-all-start.3 = ((bf16[64,1,12]{2,1,0:T(2,128)(2,1)}), bf16[64,1,12]{2,1,0:T(2,128)(2,1)S(1)}, u32[]{:S(2)}, u32[]{:S(2)}) async-start(bf16[64,1,12]{2,1,0:T(2,128)(2,1)} %copy.64), calls=%async_computation.3 | async-start | bytes 65536 | tf_op jit(solution)/shard_map/all_to_all | solution.py:117
  114.8 0.9 broadcast_in_dim_reshape.3
  115.7 5.7 %all-to-all-done.3 = bf16[64,1,12]{2,1,0:T(2,128)(2,1)S(1)} async-done(((bf16[64,1,12]{2,1,0:T(2,128)(2,1)}), bf16[64,1,12]{2,1,0:T(2,128)(2,1)S(1)}, u32[]{:S(2)}, u32[]{:S(2)}) %all-to-all-start.3) | async-done | bytes 1568 | tf_op jit(solution)/shard_map/all_to_all | solution.py:117
  121.8 1.4 %convolution_multiply_fusion = f32[8,3,2,8192]{3,0,2,1:T(8,128)S(1)} fusion(f32[8,8192]{1,0:T(8,128)S(1)} %get-tuple-element.21, f32[8,8192]{1,0:T(8,128)S(1)} %get-tuple-element.20, f32[8,8,3,2]{1,0,3,2:T(8,128)S(1)} %maximum_negate_fusion, f32[8,8,1,2]{1,0,3,2:T(8,128)S(1)} %slice_negate_fusion, f32[8,8,2,2]{1,0,3,2:T(8,128)S(1)} %slice.48), kind=kOutput, calls=%fused_computation | convolution fusion | flops 76023296 | bytes 2100224 | tf_op jit(solution)/shard_map/dot_general | solution.py:42
  123.5 1.0 maximum_bitcast_fusion
  (39 shorter events, 6.3 us)
Async XLA Ops:
  0.6 14.1 %copy-start = (bf16[1,1024,1024]{2,1,0:T(8,128)(2,1)S(1)}, bf16[1,1024,1024]{2,1,0:T(8,128)(2,1)}, u32[]{:S(2)}) copy-start(bf16[1,1024,1024]{2,1,0:T(8,128)(2,1)} %param.8) | copy-start | bytes 6291460
  7.4 13.7 %all-to-all-start = ((s32[8,1,128]{2,1,0:T(1,128)}), s32[8,1,128]{2,1,0:T(1,128)S(1)}, u32[]{:S(2)}, u32[]{:S(2)}) async-start(s32[8,1,128]{2,1,0:T(1,128)} %bitcast.4), calls=%async_computation | async-start | bytes 8192 | tf_op jit(solution)/shard_map/all_to_all | solution.py:67
  21.1 4.5 %copy-start.1 = (s32[8]{0:T(128)S(1)}, s32[8]{0:T(128)}, u32[]{:S(2)}) copy-start(s32[8]{0:T(128)} %param.11) | copy-start | bytes 100
  21.1 51.6 %all-to-all-start.1 = ((bf16[8,128,1024]{2,1,0:T(8,128)(2,1)}), bf16[8,128,1024]{2,1,0:T(8,128)(2,1)}, u32[]{:S(2)}, u32[]{:S(2)}) async-start(bf16[8,128,1024]{2,1,0:T(8,128)(2,1)} %bitcast.86), calls=%async_computation.1 | async-start | bytes 4194304 | tf_op jit(solution)/shard_map/all_to_all | solution.py:64
  72.7 4.9 %copy-start.2 = (f32[2]{0:T(128)S(1)}, f32[2]{0:T(128)}, u32[]{:S(2)}) copy-start(f32[2]{0:T(128)} %constant.64.clone) | copy-start | bytes 28
  78.3 10.1 %all-to-all-start.2 = ((bf16[8,4,8]{2,1,0:T(4,128)(2,1)}), bf16[8,4,8]{2,1,0:T(4,128)(2,1)S(1)}, u32[]{:S(2)}, u32[]{:S(2)}) async-start(bf16[8,4,8]{2,1,0:T(4,128)(2,1)} %copy.60), calls=%async_computation.2 | async-start | bytes 16384 | tf_op jit(solution)/shard_map/all_to_all | solution.py:89
  111.4 10.0 %all-to-all-start.3 = ((bf16[64,1,12]{2,1,0:T(2,128)(2,1)}), bf16[64,1,12]{2,1,0:T(2,128)(2,1)S(1)}, u32[]{:S(2)}, u32[]{:S(2)}) async-start(bf16[64,1,12]{2,1,0:T(2,128)(2,1)} %copy.64), calls=%async_computation.3 | async-start | bytes 65536 | tf_op jit(solution)/shard_map/all_to_all | solution.py:117
where the time goes:
time: 125 us
  waiting for transfers between devices  60.9 us (49%)
  starting transfers between devices  18.7 us (15%)
  blocking collectives  16.9 us (14%)
  matrix products  13.9 us (11%)
  other arithmetic  9.01 us (7%)
  local copies, waits for them, and re-layouts  4.33 us (3%)
    all_to_all x1, waiting for transfers between devices, body(): lax.all_to_all(send_rows.reshape(groups, CAP, SEG), 'blk', split_axis=0,...  46 us
    psum x1, blocking collectives, body(): lax.psum(jnp.stack(pieces, axis=2).reshape(total_cycles, mode_rows * 12),...  11.5 us
    all_to_all x1, starting transfers between devices, body(): lax.all_to_all(send_keys.reshape(groups, CAP), 'blk', split_axis=0, conca...  7.28 us
    all_to_all x1, waiting for transfers between devices, body(): lax.all_to_all(harmonics, 'blk', split_axis=0, concat_axis=2, tiled=True)  6.5 us
    all_to_all x1, waiting for transfers between devices, body(): lax.all_to_all(summed.astype(jnp.bfloat16).reshape(own_cycles, mode_rows,...  5.73 us
    all_gather x1, blocking collectives, body(): lax.all_gather(harmonics, 'lblk', axis=2, tiled=True)  5.43 us
    all_to_all x1, starting transfers between devices, body(): lax.all_to_all(send_rows.reshape(groups, CAP, SEG), 'blk', split_axis=0,...  4.47 us
    dot_general x1, matrix products, body(): jnp.dot(picked.astype(jnp.bfloat16), row_values, preferred_element_type=j...  3.63 us
  transfers between devices with their start and end apart: 4, of which 4 were waited for; matrix products, arithmetic and copies ran while one was open for 5% of the time, Pallas kernels for 0%

commit v1 on v0

v1 whole, which is shorter than its diff:
```python
import functools
import math

import jax
import jax.numpy as jnp
from jax import lax
from jax.experimental import pallas as pl
from jax.experimental.pallas import tpu as pltpu
from jax.sharding import PartitionSpec as P

NPHI = 8192
SEG = 1024
R_DEV = 8
SHELLS = 2
POS = NPHI // SEG
KEYS = SHELLS * R_DEV * POS
LANES = 128
GROUP = 2 * SHELLS * R_DEV
INNER = 2
MESH = pl.DeviceIdType.MESH
F32 = jnp.float32
BF16 = jnp.bfloat16


def split(value):
    high = value.astype(BF16)
    low = (value - high.astype(F32)).astype(BF16)
    return jnp.concatenate([high, low], axis=0)


def dot_nt(a, b):
    return lax.dot_general(a, b, (((1,), (1,)), ((), ())), preferred_element_type=F32)


def iota(shape, axis):
    return lax.broadcasted_iota(jnp.int32, shape, axis)


def kernel(
    n, nl, degrees,
    rows_hbm, owner_ref, key_ref, order_ref, table_hbm, even_hbm, odd_hbm,
    eigen_ref, cycle_ref,
    rows, table, even, odd, waves, send_y, local, recv_y, send_z, recv_z,
    send1, recv1, send2, recv2,
    load_sem, y_send, y_recv, z_send, z_recv, s1_send, s1_recv, s2_send, s2_recv,
):
    total = n * nl
    depth = n // INNER
    me_b = lax.axis_index("blk")
    me_l = lax.axis_index("lblk")
    me = me_l * n + me_b
    my_z = me_b // INNER
    my_y = me_b % INNER
    pair = my_z * INNER + (INNER - 1 - my_y)

    loads = [
        pltpu.make_async_copy(src, dst, load_sem.at[at])
        for at, (src, dst) in enumerate(
            ((rows_hbm.at[0], rows), (table_hbm.at[0], table), (even_hbm.at[0], even), (odd_hbm.at[0], odd))
        )
    ]
    for load in loads:
        load.start()

    barrier = pltpu.get_barrier_semaphore()

    def greet(step, carry):
        to = lax.rem(me + step, total)
        pl.semaphore_signal(barrier, inc=1, device_id=(lax.rem(to, n), to // n), device_id_type=MESH)
        return carry

    lax.fori_loop(1, total, greet, 0)

    keys = key_ref[...]
    owners = owner_ref[...]
    slot = (keys % POS) * (SHELLS * R_DEV) + keys // POS
    orders = order_ref[...]
    m = orders.shape[0]
    phase = (iota((m, SEG), 1) * orders) % NPHI
    angle = phase.astype(F32) * (2.0 * math.pi / NPHI)
    wave_c, wave_s = jnp.cos(angle), jnp.sin(angle)

    loads[0].wait()
    pl.semaphore_wait(barrier, total - 1)

    def partial(owner):
        chosen = jnp.where(owners == owner, slot, -1)
        one_hot = jnp.where(iota((KEYS, owners.shape[1]), 0) == chosen, 1.0, 0.0).astype(BF16)
        return jnp.dot(one_hot, rows[...], preferred_element_type=F32).astype(BF16)

    def target_z(t):
        return lax.rem(my_z + 1 + t, depth)

    def y_copy(t):
        return pltpu.make_async_remote_copy(
            src_ref=send_y.at[t], dst_ref=recv_y.at[t], send_sem=y_send.at[t], recv_sem=y_recv.at[t],
            device_id=(pair, me_l), device_id_type=MESH,
        )

    def z_copy(t):
        return pltpu.make_async_remote_copy(
            src_ref=send_z.at[t], dst_ref=recv_z.at[t], send_sem=z_send.at[t], recv_sem=z_recv.at[t],
            device_id=(target_z(t) * INNER + my_y, me_l), device_id_type=MESH,
        )

    def first(t, carry):
        send_y[t] = partial(target_z(t) * INNER + (INNER - 1 - my_y))
        y_copy(t).start()
        return carry

    lax.fori_loop(0, depth, first, 0)

    spectra = dot_nt(split(jnp.concatenate([wave_c, wave_s], axis=0)), rows[...])
    spectra = spectra[: 2 * m] + spectra[2 * m :]
    turn = ((orders * (keys % POS)) % POS).astype(F32) * (2.0 * math.pi / POS)
    turn_c, turn_s = jnp.cos(turn), jnp.sin(turn)
    turned = jnp.concatenate(
        [
            turn_c * spectra[:m] - turn_s * spectra[m:],
            turn_s * spectra[:m] + turn_c * spectra[m:],
        ],
        axis=0,
    )
    own = R_DEV * n
    place = (keys // (POS * R_DEV)) * own + owners * R_DEV + (keys // POS) % R_DEV
    spots = jnp.where(iota((SHELLS * own, keys.shape[1]), 0) == place, 1.0, 0.0).astype(BF16)
    summed = dot_nt(split(turned), spots)
    summed = (summed[: 2 * m] + summed[2 * m :]) * (1.0 / math.sqrt(NPHI))
    for j in range(m):
        send1[j, 0:1, :] = summed[j : j + 1]
        send1[j, 1:2, :] = summed[m + j : m + j + 1]

    def exchange(source, landing, send_sem, recv_sem):
        def post(step, carry):
            to = lax.rem(me + step, total)
            pltpu.make_async_remote_copy(
                src_ref=source(to), dst_ref=landing.at[me], send_sem=send_sem, recv_sem=recv_sem,
                device_id=(lax.rem(to, n), to // n), device_id_type=MESH,
            ).start()
            return carry

        lax.fori_loop(1, total, post, 0)
        pltpu.make_async_copy(source(me), landing.at[me], recv_sem).start()

    def drain(landing, sem, count):
        part = landing.at[pl.ds(0, count)]
        pltpu.make_async_copy(part, part, sem).wait()

    exchange(lambda to: send1.at[lax.rem(to, n)], recv1, s1_send, s1_recv)

    def second(t, carry):
        local[t] = partial(target_z(t) * INNER + my_y)
        return carry

    lax.fori_loop(0, depth, second, 0)

    width = table.shape[0]
    degree = (me_l * width + iota((1, width), 1)).astype(F32)
    smoothing = jnp.exp(-2.0 * degree * (degree + 1.0) / (degrees * degrees))
    factor = jnp.sqrt(
        jnp.maximum((degree - 1.0) * (degree + 2.0), 0.0) / jnp.maximum(degree * (degree + 1.0), 1.0)
    )
    shear = -0.5 * smoothing * factor
    for load in loads[1:]:
        load.wait()

    def forward(t):
        y_copy(t).wait_recv()
        send_z[t] = (local[t].astype(F32) + recv_y[t].astype(F32)).astype(BF16)
        z_copy(t).start()

    drain(recv1, s1_recv, total)
    line = iota((3 * GROUP, 1), 0)
    comp = line // GROUP
    part = (line // (SHELLS * R_DEV)) % 2
    shell = (line // R_DEV) % SHELLS
    from_sine = jnp.where(comp == 2, 1 - part, part) == 1
    sign = jnp.where((comp == 2) & (part == 1), -1.0, 1.0)
    blocks = []
    for q in range(nl):
        got = jnp.sum(recv1[q * n : (q + 1) * n], axis=0)
        cosine, sine = got[0:1], got[1:2]
        blocks.append(
            sign
            * jnp.where(
                from_sine,
                jnp.where(shell == 0, sine[:, :own], sine[:, own:]),
                jnp.where(shell == 0, cosine[:, :own], cosine[:, own:]),
            )
        )
    harmonics = jnp.concatenate(blocks, axis=1).astype(BF16)
    coefficients = dot_nt(harmonics, table[...])
    trace_terms = (coefficients[:GROUP] * smoothing).astype(BF16)
    shear_terms = (coefficients[GROUP:] * shear).astype(BF16)
    synthesis = jnp.concatenate(
        [
            jnp.dot(trace_terms, table[...], preferred_element_type=F32),
            jnp.dot(shear_terms[:GROUP], even[...], preferred_element_type=F32),
            jnp.dot(shear_terms[GROUP:], odd[...], preferred_element_type=F32),
            jnp.zeros((LANES - 3 * GROUP, table.shape[1]), F32),
        ],
        axis=0,
    )
    send2[...] = synthesis.T.reshape(total, R_DEV, LANES)
    exchange(lambda to: send2.at[to], recv2, s2_send, s2_recv)

    forward(0)

    for p in range(POS):
        turn = ((orders * p) % POS).astype(F32) * (2.0 * math.pi / POS)
        turn_c, turn_s = jnp.cos(turn), jnp.sin(turn)
        waves[:, p * SEG : (p + 1) * SEG] = split(
            jnp.concatenate(
                [turn_c * wave_c - turn_s * wave_s, turn_s * wave_c + turn_c * wave_s], axis=0
            )
        )

    if depth > 2:
        forward(1)

    drain(recv2, s2_recv, total)
    got = recv2[0:n]
    for q in range(1, nl):
        got = got + recv2[q * n : (q + 1) * n]
    own_line = iota(got.shape, 2) % R_DEV == iota(got.shape, 1)
    modes = jnp.sum(jnp.where(own_line, got, 0.0), axis=1).T
    halves = SHELLS * R_DEV
    sides = [
        jnp.concatenate(
            [modes[g * GROUP + c * halves : g * GROUP + (c + 1) * halves] for g in range(3)], axis=0
        )
        for c in range(2)
    ]
    stacked = jnp.concatenate(sides + sides, axis=1).astype(BF16)
    scale = 2.0 / math.sqrt(m)
    for p in range(POS):
        span = pl.ds(p * SEG, SEG)
        fields = jnp.dot(stacked, waves[:, span], preferred_element_type=F32) * scale
        half_trace = 0.5 * fields[:halves]
        first_part, second_part = fields[halves : 2 * halves], fields[2 * halves :]
        size = jnp.sqrt(first_part * first_part + second_part * second_part)
        for at, value in enumerate((half_trace + size, half_trace - size)):
            for s in range(SHELLS):
                eigen_ref[at, s, 0, :, span] = value[s * R_DEV : (s + 1) * R_DEV]

    def rest(t, carry):
        forward(t)
        return carry

    lax.fori_loop(min(2, depth - 1), depth - 1, rest, 0)

    y_copy(depth - 1).wait_recv()

    def landed(t, carry):
        z_copy(t).wait_recv()
        return carry

    lax.fori_loop(0, depth - 1, landed, 0)
    for p in range(POS):
        lines = pl.ds(p * halves, halves)

        def add(t, value):
            return value + recv_z[t, lines, :].astype(F32)

        value = local[depth - 1, lines, :].astype(F32) + recv_y[depth - 1, lines, :].astype(F32)
        value = lax.fori_loop(0, depth - 1, add, value)
        for s in range(SHELLS):
            cycle_ref[s, 0, :, pl.ds(p * SEG, SEG)] = value[s * R_DEV : (s + 1) * R_DEV]

    def sent_y(t, carry):
        y_copy(t).wait_send()
        return carry

    def sent_z(t, carry):
        z_copy(t).wait_send()
        return carry

    lax.fori_loop(0, depth, sent_y, 0)
    lax.fori_loop(0, depth - 1, sent_z, 0)
    drain(recv1, s1_send, total - 1)
    drain(recv2, s2_send, total - 1)


def body(partial_rows, row_owner, row_key, azimuth_orders, legendre_table, spin_even, spin_odd):
    n = lax.axis_size("blk")
    nl = lax.axis_size("lblk")
    total = n * nl
    depth = n // INNER
    count = partial_rows.shape[1]
    m = azimuth_orders.shape[0]
    width, cycles = legendre_table.shape[1:]
    block = (KEYS, SEG)
    vmem = pl.BlockSpec(memory_space=pltpu.VMEM)
    hbm = pl.BlockSpec(memory_space=pl.ANY)
    lanes = SHELLS * R_DEV * n
    dma = pltpu.SemaphoreType.DMA
    return pl.pallas_call(
        functools.partial(kernel, n, nl, float(width * nl)),
        out_shape=(
            jax.ShapeDtypeStruct((2, SHELLS, 1, R_DEV, NPHI), F32),
            jax.ShapeDtypeStruct((SHELLS, 1, R_DEV, NPHI), F32),
        ),
        in_specs=[hbm, vmem, vmem, vmem, hbm, hbm, hbm],
        out_specs=(vmem, vmem),
        scratch_shapes=[
            pltpu.VMEM((count, SEG), BF16),
            pltpu.VMEM((width, cycles), BF16),
            pltpu.VMEM((width, cycles), BF16),
            pltpu.VMEM((width, cycles), BF16),
            pltpu.VMEM((4 * m, NPHI), BF16),
            pltpu.VMEM((depth, *block), BF16),
            pltpu.VMEM((depth, *block), BF16),
            pltpu.VMEM((depth, *block), BF16),
            pltpu.VMEM((depth - 1, *block), BF16),
            pltpu.VMEM((depth - 1, *block), BF16),
            pltpu.VMEM((m, 2, lanes), F32),
            pltpu.VMEM((total, 2, lanes), F32),
            pltpu.VMEM((total, R_DEV, LANES), F32),
            pltpu.VMEM((total, R_DEV, LANES), F32),
            dma((4,)),
            dma((depth,)),
            dma((depth,)),
            dma((depth - 1,)),
            dma((depth - 1,)),
            dma,
            dma,
            dma,
            dma,
        ],
        compiler_params=pltpu.CompilerParams(
            collective_id=0, has_side_effects=True, vmem_limit_bytes=52 * 2**20
        ),
        cost_estimate=pl.CostEstimate(flops=6 * 10**9, bytes_accessed=6 * 10**6, transcendentals=10**5),
    )(
        partial_rows,
        row_owner.reshape(1, count),
        row_key,
        azimuth_orders.reshape(m, 1),
        legendre_table,
        spin_even,
        spin_odd,
    )


def solution(mesh):
    return jax.shard_map(
        body,
        mesh=mesh,
        in_specs=(
            P("lblk", "blk", None),
            P("lblk", "blk", None),
            P("lblk", "blk"),
            P(),
            P("blk", "lblk", None),
            P("blk", "lblk", None),
            P("blk", "lblk", None),
        ),
        out_specs=(P(None, None, "lblk", "blk", None), P(None, "lblk", "blk", None)),
        check_vma=False,
    )
```

time: 125 us -> 69.5 us (0.56)
  Pallas kernels: 0 us -> 61.2 us
  waiting for transfers between devices: 60.9 us -> 0 us
  starting transfers between devices: 18.7 us -> 0 us
  blocking collectives: 16.9 us -> 0 us
  matrix products: 13.9 us -> 0 us
  other arithmetic: 9.01 us -> 0 us
  local copies, waits for them, and re-layouts: 4.33 us -> 7.24 us
    pallas_call x0 -> x1, Pallas kernels: none -> 61.2 us  [body(): pl.pallas_call(functools.partial(kernel, n, nl, float(width * nl)), out_s...]
    all_to_all x4 -> x0, waiting for transfers between devices: 60.9 us -> none  [the longest x1 46 us: body(): lax.all_to_all(send_rows.reshape(groups, CAP, SEG), 'blk', split_axis=0,...]
    all_to_all x4 -> x0, starting transfers between devices: 18.7 us -> none  [the longest x1 7.28 us: body(): lax.all_to_all(send_keys.reshape(groups, CAP), 'blk', split_axis=0, conca...]
    dot_general x8 -> x0, matrix products: 13.9 us -> none  [the longest x1 3.63 us: body(): jnp.dot(picked.astype(jnp.bfloat16), row_values, preferred_element_type=j...]
    psum x1 -> x0, blocking collectives: 11.5 us -> none  [body(): lax.psum(jnp.stack(pieces, axis=2).reshape(total_cycles, mode_rows * 12),...]
    unnamed x8 -> x10, local copies, waits for them, and re-layouts: 0.16 us -> 6.51 us
    all_gather x1 -> x0, blocking collectives: 5.43 us -> none  [body(): lax.all_gather(harmonics, 'lblk', axis=2, tiled=True)]
    another operation x3 -> x0, other arithmetic: 2.42 us -> none
  transfers between devices with their start and end apart: 4 -> 0, of which waited for: 4 -> 0; matrix products, arithmetic and copies ran while one was open for 5% -> 0% of each run, Pallas kernels for 0% -> 0%
where the time goes in v1:
time: 69.5 us; the launch traced here: 69.1 us
  Pallas kernels  61.2 us (88%)
  local copies, waits for them, and re-layouts  7.24 us (10%)
    pallas_call x1, Pallas kernels, body(): pl.pallas_call(functools.partial(kernel, n, nl, float(width * nl)), out_s...  61.2 us
    unnamed x10, local copies, waits for them, and re-layouts  6.51 us

profile of v1, /device:TPU:0, one launch (start us, length us, event | category | flops | bytes accessed | tf_op | source)
XLA Modules:
  0.0 69.1 jit_solution(1919847996177764124)
XLA Ops:
  0.6 0.7 %copy.9.order_ref = s32[8,1]{1,0:T(8,128)S(1)} copy(s32[8,1]{0,1:T(1,128)} %bitcast.3) | data formatting | bytes 64 | tf_op jit(solution)/shard_map/reshape | solution.py:338
  1.4 0.0 copy-start
  1.4 1.0 %copy-done = bf16[1,1024,256]{2,1,0:T(8,128)(2,1)S(1)} copy-done((bf16[1,1024,256]{2,1,0:T(8,128)(2,1)S(1)}, bf16[1,1024,256]{2,1,0:T(8,128)(2,1)}, u32[]{:S(2)}) %copy-start) | copy-done | bytes 524312
  2.4 0.0 copy-start.1
  2.4 1.0 %copy-done.1 = bf16[1,1024,256]{2,1,0:T(8,128)(2,1)S(1)} copy-done((bf16[1,1024,256]{2,1,0:T(8,128)(2,1)S(1)}, bf16[1,1024,256]{2,1,0:T(8,128)(2,1)}, u32[]{:S(2)}) %copy-start.1) | copy-done | bytes 524312
  3.4 0.0 copy-start.2
  3.4 0.7 copy-done.2
  4.1 0.0 copy-start.3
  4.1 0.7 copy-done.3
  4.8 61.2 %shard_map.86 = (f32[2,2,1,8,8192]{4,3,2,1,0:T(8,128)}, f32[2,1,8,8192]{3,2,1,0:T(8,128)S(1)}) custom-call(bf16[1,1024,1024]{2,1,0:T(8,128)(2,1)} %rows_hbm.1, s32[1,1024]{1,0:T(1,128)S(1)} %bitcast.2, s32[1,1024]{1,0:T(1,128)S(1)} %copy-done.3, s32[8,1]{1,0:T(8,128)S(1)} %copy.9.order_ref, bf16[1,1024,256]{2,1,0:T(8,128)(2,1)S(1)} %copy-done, ...), custom_call_target="tpu_custom_call" | custom-call | flops 6000000000 | bytes 6000000 | tf_op jit(solution)/shard_map/pallas_call | solution.py:297
  66.0 2.3 %copy.12 = f32[2,2,1,8,8192]{4,3,2,1,0:T(8,128)} copy(f32[2,2,1,8,8192]{4,3,2,1,0:T(8,128)} %get-tuple-element.4) | data formatting | bytes 2097152
  68.3 0.8 %copy.13 = f32[2,1,8,8192]{3,2,1,0:T(8,128)} copy(f32[2,1,8,8192]{3,2,1,0:T(8,128)S(1)} %get-tuple-element.5) | data formatting | bytes 1048576
Async XLA Ops:
  1.4 1.0 %copy-start = (bf16[1,1024,256]{2,1,0:T(8,128)(2,1)S(1)}, bf16[1,1024,256]{2,1,0:T(8,128)(2,1)}, u32[]{:S(2)}) copy-start(bf16[1,1024,256]{2,1,0:T(8,128)(2,1)} %table_hbm.1) | copy-start | bytes 1572868
  2.4 1.0 %copy-start.1 = (bf16[1,1024,256]{2,1,0:T(8,128)(2,1)S(1)}, bf16[1,1024,256]{2,1,0:T(8,128)(2,1)}, u32[]{:S(2)}) copy-start(bf16[1,1024,256]{2,1,0:T(8,128)(2,1)} %even_hbm.1) | copy-start | bytes 1572868
  3.4 0.7 copy-start.2
  4.1 0.7 copy-start.3

commit v2 on v1

--- a/solution.py
+++ b/solution.py
@@ -38,9 +38,9 @@
 
 def kernel(
     n, nl, degrees,
-    rows_hbm, owner_ref, key_ref, order_ref, table_hbm, even_hbm, odd_hbm,
+    rows_hbm, owner_hbm, key_hbm, order_hbm, table_hbm, even_hbm, odd_hbm,
     eigen_ref, cycle_ref,
-    rows, table, even, odd, waves, send_y, local, recv_y, send_z, recv_z,
+    owner_ref, key_ref, order_ref, rows, table, even, odd, waves, send_y, local, recv_y, send_z, recv_z,
     send1, recv1, send2, recv2,
     load_sem, y_send, y_recv, z_send, z_recv, s1_send, s1_recv, s2_send, s2_recv,
 ):
@@ -56,7 +56,7 @@
     loads = [
         pltpu.make_async_copy(src, dst, load_sem.at[at])
         for at, (src, dst) in enumerate(
-            ((rows_hbm.at[0], rows), (table_hbm.at[0], table), (even_hbm.at[0], even), (odd_hbm.at[0], odd))
+            ((order_hbm, order_ref), (key_hbm, key_ref), (owner_hbm, owner_ref), (rows_hbm.at[0], rows), (table_hbm.at[0], table), (even_hbm.at[0], even), (odd_hbm.at[0], odd))
         )
     ]
     for load in loads:
@@ -71,17 +71,15 @@
 
     lax.fori_loop(1, total, greet, 0)
 
+    for load in loads[:3]:
+        load.wait()
     keys = key_ref[...]
     owners = owner_ref[...]
     slot = (keys % POS) * (SHELLS * R_DEV) + keys // POS
-    orders = order_ref[...]
-    m = orders.shape[0]
-    phase = (iota((m, SEG), 1) * orders) % NPHI
-    angle = phase.astype(F32) * (2.0 * math.pi / NPHI)
-    wave_c, wave_s = jnp.cos(angle), jnp.sin(angle)
-
-    loads[0].wait()
-    pl.semaphore_wait(barrier, total - 1)
+    m = order_ref.shape[1]
+    spread = jnp.where(iota((m, m), 0) == iota((m, m), 1), order_ref[...].astype(F32), 0.0)
+    orders = jnp.sum(spread, axis=1, keepdims=True).astype(jnp.int32)
+    loads[3].wait()
 
     def partial(owner):
         chosen = jnp.where(owners == owner, slot, -1)
@@ -108,12 +106,21 @@
         y_copy(t).start()
         return carry
 
-    lax.fori_loop(0, depth, first, 0)
-
+    pl.semaphore_wait(barrier, total - 1)
+    lead, early = 0, min(1, depth)
+    lax.fori_loop(0, lead, first, 0)
+    phase = (iota((m, SEG), 1) * orders) % NPHI
+    angle = phase.astype(F32) * (2.0 * math.pi / NPHI)
+    wave_c, wave_s = jnp.cos(angle), jnp.sin(angle)
+    eighth = ((iota((m, LANES), 1) * orders) % POS).astype(F32) * (2.0 * math.pi / POS)
+    eighth_c, eighth_s = jnp.cos(eighth), jnp.sin(eighth)
     spectra = dot_nt(split(jnp.concatenate([wave_c, wave_s], axis=0)), rows[...])
     spectra = spectra[: 2 * m] + spectra[2 * m :]
-    turn = ((orders * (keys % POS)) % POS).astype(F32) * (2.0 * math.pi / POS)
-    turn_c, turn_s = jnp.cos(turn), jnp.sin(turn)
+    turn_c, turn_s = jnp.zeros((m, keys.shape[1]), F32), jnp.zeros((m, keys.shape[1]), F32)
+    for p in range(POS):
+        here = keys % POS == p
+        turn_c = jnp.where(here, eighth_c[:, p : p + 1], turn_c)
+        turn_s = jnp.where(here, eighth_s[:, p : p + 1], turn_s)
     turned = jnp.concatenate(
         [
             turn_c * spectra[:m] - turn_s * spectra[m:],
@@ -147,6 +154,7 @@
         pltpu.make_async_copy(part, part, sem).wait()
 
     exchange(lambda to: send1.at[lax.rem(to, n)], recv1, s1_send, s1_recv)
+    lax.fori_loop(lead, early, first, 0)
 
     def second(t, carry):
         local[t] = partial(target_z(t) * INNER + my_y)
@@ -161,7 +169,7 @@
         jnp.maximum((degree - 1.0) * (degree + 2.0), 0.0) / jnp.maximum(degree * (degree + 1.0), 1.0)
     )
     shear = -0.5 * smoothing * factor
-    for load in loads[1:]:
+    for load in loads[4:]:
         load.wait()
 
     def forward(t):
@@ -203,21 +211,23 @@
     )
     send2[...] = synthesis.T.reshape(total, R_DEV, LANES)
     exchange(lambda to: send2.at[to], recv2, s2_send, s2_recv)
+    lax.fori_loop(early, depth, first, 0)
 
     forward(0)
 
     for p in range(POS):
-        turn = ((orders * p) % POS).astype(F32) * (2.0 * math.pi / POS)
-        turn_c, turn_s = jnp.cos(turn), jnp.sin(turn)
+        turn_c, turn_s = eighth_c[:, p : p + 1], eighth_s[:, p : p + 1]
         waves[:, p * SEG : (p + 1) * SEG] = split(
             jnp.concatenate(
                 [turn_c * wave_c - turn_s * wave_s, turn_s * wave_c + turn_c * wave_s], axis=0
             )
         )
 
-    if depth > 2:
-        forward(1)
-
+    def rest(t, carry):
+        forward(t)
+        return carry
+
+    lax.fori_loop(1, depth - 1, rest, 0)
     drain(recv2, s2_recv, total)
     got = recv2[0:n]
     for q in range(1, nl):
@@ -243,12 +253,6 @@
             for s in range(SHELLS):
                 eigen_ref[at, s, 0, :, span] = value[s * R_DEV : (s + 1) * R_DEV]
 
-    def rest(t, carry):
-        forward(t)
-        return carry
-
-    lax.fori_loop(min(2, depth - 1), depth - 1, rest, 0)
-
     y_copy(depth - 1).wait_recv()
 
     def landed(t, carry):
@@ -291,7 +295,7 @@
     width, cycles = legendre_table.shape[1:]
     block = (KEYS, SEG)
     vmem = pl.BlockSpec(memory_space=pltpu.VMEM)
-    hbm = pl.BlockSpec(memory_space=pl.ANY)
+    hbm = pl.BlockSpec(memory_space=pltpu.HBM)
     lanes = SHELLS * R_DEV * n
     dma = pltpu.SemaphoreType.DMA
     return pl.pallas_call(
@@ -300,9 +304,12 @@
             jax.ShapeDtypeStruct((2, SHELLS, 1, R_DEV, NPHI), F32),
             jax.ShapeDtypeStruct((SHELLS, 1, R_DEV, NPHI), F32),
         ),
-        in_specs=[hbm, vmem, vmem, vmem, hbm, hbm, hbm],
+        in_specs=[hbm] * 7,
         out_specs=(vmem, vmem),
         scratch_shapes=[
+            pltpu.VMEM((1, count), jnp.int32),
+            pltpu.VMEM((1, count), jnp.int32),
+            pltpu.VMEM((1, m), jnp.int32),
             pltpu.VMEM((count, SEG), BF16),
             pltpu.VMEM((width, cycles), BF16),
             pltpu.VMEM((width, cycles), BF16),
@@ -317,7 +324,7 @@
             pltpu.VMEM((total, 2, lanes), F32),
             pltpu.VMEM((total, R_DEV, LANES), F32),
             pltpu.VMEM((total, R_DEV, LANES), F32),
-            dma((4,)),
+            dma((7,)),
             dma((depth,)),
             dma((depth,)),
             dma((depth - 1,)),
@@ -328,14 +335,14 @@
             dma,
         ],
         compiler_params=pltpu.CompilerParams(
-            collective_id=0, has_side_effects=True, vmem_limit_bytes=52 * 2**20
+            collective_id=0, has_side_effects=True, vmem_limit_bytes=62 * 2**20
         ),
         cost_estimate=pl.CostEstimate(flops=6 * 10**9, bytes_accessed=6 * 10**6, transcendentals=10**5),
     )(
         partial_rows,
         row_owner.reshape(1, count),
         row_key,
-        azimuth_orders.reshape(m, 1),
+        azimuth_orders.reshape(1, m),
         legendre_table,
         spin_even,
         spin_odd,

time: 69.5 us -> 46.4 us (0.67)
  Pallas kernels: 61.2 us -> 42.5 us
  local copies, waits for them, and re-layouts: 7.24 us -> 3.12 us
    pallas_call x1, Pallas kernels: 61.2 us -> 42.5 us  [body(): pl.pallas_call(functools.partial(kernel, n, nl, float(width * nl)), out_s...]
    unnamed x10 -> x4, local copies, waits for them, and re-layouts: 6.51 us -> 3.12 us
    reshape x1 -> x0, local copies, waits for them, and re-layouts: 0.73 us -> none  [body(): azimuth_orders.reshape(m, 1)]
where the time goes in v2:
time: 46.4 us; the launch traced here: 46.2 us
  Pallas kernels  42.5 us (92%)
  local copies, waits for them, and re-layouts  3.12 us (7%)
  between operations  0.65 us (1%)
    pallas_call x1, Pallas kernels, body(): pl.pallas_call(functools.partial(kernel, n, nl, float(width * nl)), out_s...  42.5 us
    unnamed x4, local copies, waits for them, and re-layouts  3.12 us

profile of v2, /device:TPU:0, one launch (start us, length us, event | category | flops | bytes accessed | tf_op | source)
XLA Modules:
  0.0 46.2 jit_solution(3101571153305958504)
XLA Ops:
  0.6 42.5 %shard_map.86 = (f32[2,2,1,8,8192]{4,3,2,1,0:T(8,128)}, f32[2,1,8,8192]{3,2,1,0:T(8,128)}) custom-call(bf16[1,1024,1024]{2,1,0:T(8,128)(2,1)} %rows_hbm.1, s32[1,1024]{1,0:T(1,128)} %bitcast.2, s32[1,1024]{1,0:T(1,128)} %key_hbm.1, s32[1,8]{1,0:T(1,128)} %bitcast.3, bf16[1,1024,256]{2,1,0:T(8,128)(2,1)} %table_hbm.1, bf16[1,1024,256]{2,1,0:T(8,128)(2,1)} %even_hbm.1, ...), custom_call_target="tpu_custom_call" | custom-call | flops 6000000000 | bytes 6000000 | tf_op jit(solution)/shard_map/pallas_call | solution.py:301
  43.1 0.0 copy-start
  43.1 2.3 %copy.11 = f32[2,2,1,8,8192]{4,3,2,1,0:T(8,128)} copy(f32[2,2,1,8,8192]{4,3,2,1,0:T(8,128)} %get-tuple-element.4) | data formatting | bytes 2097152
  45.4 0.0 copy-done
  45.4 0.8 %copy.12 = f32[2,1,8,8192]{3,2,1,0:T(8,128)} copy(f32[2,1,8,8192]{3,2,1,0:T(8,128)S(1)} %copy-done) | data formatting | bytes 1048576
Async XLA Ops:
  43.1 2.3 %copy-start = (f32[2,1,8,8192]{3,2,1,0:T(8,128)S(1)}, f32[2,1,8,8192]{3,2,1,0:T(8,128)}, u32[]{:S(2)}) copy-start(f32[2,1,8,8192]{3,2,1,0:T(8,128)} %get-tuple-element.5) | copy-start | bytes 1572868
